TPU v7x, 512 devices: a whole 4x8x8 slice. The times are simulated.
512 devices in a mesh: rep: 2 (over x_hi), ty: 16 (over z, core), tx: 16 (over x_lo, y).
Axes of the slice: x: 4 (x_hi: 2, x_lo: 2; x = x_hi * 2 + x_lo), y: 8, z: 8, core: 2. Of those that a mesh axis runs over, the one named last changes fastest.
Arguments:
- state: float32 [2, 32, 80, 2048], P('rep', 'ty', None, 'tx'), may hold values from -6 to 6
- kappa: float32 [32, 2048], P('ty', 'tx'), may hold values from 0.02 to 0.12
- tile_face: int32 [16, 16], P('ty', 'tx'), may hold values from 0 to 5
- seam_turn: int32 [16, 16, 4], P('ty', 'tx'), may hold values from 0 to 3
- face_rate: float32 [6, 80], replicated, may hold values from 0.5 to 2
- w_in: bfloat16 [80, 512], replicated, may hold values from -0.625 to 0.625
- bias_in: float32 [512], replicated, may hold values from -6 to 6
- w_out: bfloat16 [512, 80], replicated, may hold values from -0.09375 to 0.09375
- cotangent: float32 [2, 32, 80, 2048], P('rep', 'ty', None, 'tx'), may hold values from -12 to 12
Outputs:
- final_state: float32 [2, 32, 80, 2048], P('rep', 'ty', None, 'tx')
- state_grad: float32 [2, 32, 80, 2048], P('rep', 'ty', None, 'tx')
- grad_w_in: float32 [80, 512], replicated
- grad_w_out: float32 [512, 80], replicated
- grad_bias: float32 [512], replicated
Inputs may be any that keep to these rules, and one draw needn't show every extreme that they name: `seam_turn`: rotation code of each tile edge, in quarter turns, as the steps define it.
All inputs are finite; a program needn't handle non-finite values.
Results may differ from a plain program's by a relative error of at most 0.0035.
Values sent between devices are 32-bit elements; how exact they have to be, the bound alone decides.
A program may use at most 64 MiB of HBM per device.

v0:
```python
import math

import jax
import jax.numpy as jnp
from jax import lax
from jax.sharding import PartitionSpec as P

LEV = 16
SUBSTEPS = 4


def extended(value, sides, width):
    for axis, dim in sides:
        devices, length = (lax.axis_size(axis), value.shape[dim])
        up = [(i, (i + 1) % devices) for i in range(devices)]
        down = [(j, i) for i, j in up]
        last = lax.slice_in_dim(value, length - width, length, axis=dim)
        first = lax.slice_in_dim(value, 0, width, axis=dim)
        before = lax.ppermute(last, axis, up)
        after = lax.ppermute(first, axis, down)
        value = jnp.concatenate([before, value, after], axis=dim)
    return value


def turn_strip(edge_strip, turn_code, inverse):
    reverse = (turn_code == 1) | (turn_code == 2)
    edge_strip = jnp.where(reverse, jnp.flip(edge_strip, -1), edge_strip)
    cosine = (turn_code == 0).astype(jnp.float32) - (turn_code == 2).astype(jnp.float32)
    sine_part = (turn_code == 1).astype(jnp.float32) - (turn_code == 3).astype(jnp.float32)
    if inverse:
        sine_part = -sine_part
    zonal_wind = edge_strip[..., :LEV, :]
    meridional = edge_strip[..., LEV : 2 * LEV, :]
    others = edge_strip[..., 2 * LEV :, :]
    return jnp.concatenate(
        [
            cosine * zonal_wind - sine_part * meridional,
            sine_part * zonal_wind + cosine * meridional,
            others,
        ],
        axis=-2,
    )


def stencil_sum(field, northern, southern, western, eastern):
    from_above = jnp.concatenate([northern[..., None, :, :], field[..., :-1, :, :]], axis=-3)
    from_below = jnp.concatenate([field[..., 1:, :, :], southern[..., None, :, :]], axis=-3)
    from_left = jnp.concatenate(
        [jnp.swapaxes(western, -1, -2)[..., None], field[..., :-1]], axis=-1
    )
    from_right = jnp.concatenate(
        [field[..., 1:], jnp.swapaxes(eastern, -1, -2)[..., None]], axis=-1
    )
    return from_above + from_below + from_left + from_right - 4.0 * field


def laplace(field, turns):
    padded = extended(field[None], (("ty", 1), ("tx", 3)), 1)[0]
    northern = turn_strip(padded[0, :, 1:-1], turns[0], False)
    southern = turn_strip(padded[-1, :, 1:-1], turns[1], False)
    western = turn_strip(padded[1:-1, :, 0].T, turns[2], False)
    eastern = turn_strip(padded[1:-1, :, -1].T, turns[3], False)
    return stencil_sum(field, northern, southern, western, eastern)


def laplace_adjoint(weighted, turns):
    rows, channels, width = weighted.shape
    zero_row = jnp.zeros((channels, width), jnp.float32)
    zero_col = jnp.zeros((channels, rows), jnp.float32)
    local = stencil_sum(weighted, zero_row, zero_row, zero_col, zero_col)
    back_north = turn_strip(weighted[0], turns[0], True)
    back_south = turn_strip(weighted[-1], turns[1], True)
    back_west = turn_strip(weighted[:, :, 0].T, turns[2], True)
    back_east = turn_strip(weighted[:, :, -1].T, turns[3], True)
    edge_rows = jnp.stack([back_north, back_south], axis=0)[None]
    got_rows = extended(edge_rows, (("ty", 1),), 1)[0]
    edge_cols = jnp.stack([back_west.T, back_east.T], axis=2)[None]
    got_cols = extended(edge_cols, (("tx", 3),), 1)[0]
    from_north = got_rows[0]
    from_south = got_rows[3]
    from_west = got_cols[:, :, 0]
    from_east = got_cols[:, :, 3]
    local = local.at[0].add(from_north).at[-1].add(from_south)
    local = local.at[:, :, 0].add(from_west).at[:, :, -1].add(from_east)
    return local


def column_forward(inputs, w_in, bias_in, w_out):
    hidden_z = (
        jnp.einsum("ch,ycx->yhx", w_in, inputs, preferred_element_type=jnp.float32)
        + bias_in[None, :, None]
    )
    hidden = (hidden_z * jax.nn.sigmoid(hidden_z)).astype(jnp.bfloat16)
    return jnp.einsum("hc,yhx->ycx", w_out, hidden, preferred_element_type=jnp.float32)


def column_backward(inputs, grad_cols, w_in, bias_in, w_out):
    hidden_z = (
        jnp.einsum("ch,ycx->yhx", w_in, inputs, preferred_element_type=jnp.float32)
        + bias_in[None, :, None]
    )
    squashed = jax.nn.sigmoid(hidden_z)
    hidden = (hidden_z * squashed).astype(jnp.bfloat16)
    cot_b = grad_cols.astype(jnp.bfloat16)
    gate_grad = (
        jnp.einsum("hc,ycx->yhx", w_out, cot_b, preferred_element_type=jnp.float32)
        * squashed
        * (1.0 + hidden_z * (1.0 - squashed))
    )
    gate_b = gate_grad.astype(jnp.bfloat16)
    dw_in = jnp.einsum("ycx,yhx->ch", inputs, gate_b, preferred_element_type=jnp.float32)
    dw_out = jnp.einsum("yhx,ycx->hc", hidden, cot_b, preferred_element_type=jnp.float32)
    dbias = jnp.sum(gate_grad, axis=(0, 2))
    back = jnp.einsum("ch,yhx->ycx", w_in, gate_b, preferred_element_type=jnp.float32)
    return (dw_in, dw_out, dbias, back)


def shards(state, kappa, tile_face, seam_turn, face_rate, w_in, bias_in, w_out, cotangent):
    rows, width = (state.shape[1], state.shape[3])
    turns = seam_turn[0, 0]
    face_mask = (jnp.arange(face_rate.shape[0]) == tile_face[0, 0]).astype(jnp.float32)
    rate = jnp.dot(face_mask, face_rate, precision=lax.Precision.HIGHEST)
    coef = kappa[:, None, :] * rate[None, :, None]
    field = state[0]
    saved = []
    for substep in range(SUBSTEPS):
        pre = field + coef * laplace(field, turns)
        inputs = pre.astype(jnp.bfloat16)
        field = pre + column_forward(inputs, w_in, bias_in, w_out)
        saved.append(inputs)
    grad = cotangent[0]
    total_in = jnp.zeros(w_in.shape, jnp.float32)
    total_out = jnp.zeros(w_out.shape, jnp.float32)
    total_bias = jnp.zeros(bias_in.shape, jnp.float32)
    for substep in reversed(range(SUBSTEPS)):
        dw_in, dw_out, dbias, back = column_backward(saved[substep], grad, w_in, bias_in, w_out)
        pre_grad = grad + back
        grad = pre_grad + laplace_adjoint(coef * pre_grad, turns)
        total_in = total_in + dw_in
        total_out = total_out + dw_out
        total_bias = total_bias + dbias
    total_in, total_out, total_bias = lax.psum(
        (total_in, total_out, total_bias), ("rep", "ty", "tx")
    )
    all_columns = lax.axis_size("rep") * lax.axis_size("ty") * lax.axis_size("tx") * rows * width
    factor = 1.0 / math.sqrt(all_columns)
    return (field[None], grad[None], total_in * factor, total_out * factor, total_bias * factor)


def solution(mesh):
    placed = (
        P("rep", "ty", None, "tx"),
        P("ty", "tx"),
        P("ty", "tx"),
        P("ty", "tx", None),
        P(),
        P(),
        P(),
        P(),
        P("rep", "ty", None, "tx"),
    )
    return jax.shard_map(
        shards,
        mesh=mesh,
        in_specs=placed,
        out_specs=(P("rep", "ty", None, "tx"), P("rep", "ty", None, "tx"), P(), P(), P()),
        check_vma=False,
    )
```

profile of v0, /device:TPU:1, one launch (start us, length us, event | category | flops | bytes accessed | tf_op | source)
XLA Modules:
  0.0 537.6 jit_solution(12932477868638475645)
XLA Ops:
  7.2 0.8 slice_bitcast_fusion.9
  8.1 3.5 collective-permute-start
  11.6 3.4 collective-permute-start.1
  15.0 0.6 fusion.115
  27.1 2.6 collective-permute-start.3
  29.7 2.7 collective-permute-start.2
  32.4 0.7 collective-permute-done.3
  33.1 4.7 collective-permute-done.2
  39.4 0.7 copy-done.5
  40.3 0.5 copy-done.8
  41.1 0.5 copy-done.2
  41.9 8.0 %collective-permute-start.5 = (f32[1,1,80,128]{3,2,1,0:T(8,128)S(1)}, f32[1,1,80,128]{3,2,1,0:T(8,128)S(1)}, u32[]{:S(2)}, u32[]{:S(2)}) collective-permute-start(f32[1,1,80,128]{3,2,1,0:T(8,128)S(1)} %get-tuple-element.304), channel_id=1, source_target_pairs={{16,0},{32,16},{48,32},{64,48},{80,64},{96,80},{112,96},{128,112},... | collective-permute-start | bytes 122888 | tf_op jit(solution)/shard_map/ppermute | solution.py:20
  50.0 0.8 collective-permute-done.5
  51.2 1.9 collective-permute-start.7
  53.1 3.4 collective-permute-start.6
  56.5 0.7 collective-permute-done.7
  57.3 4.0 collective-permute-done.6
  63.1 1.1 multiply_convert_fusion.2
  64.4 4.6 collective-permute-start.9
  69.1 0.8 collective-permute-done.9
  70.3 1.9 collective-permute-start.11
  72.2 3.4 collective-permute-start.10
  75.6 0.7 collective-permute-done.11
  76.4 4.0 collective-permute-done.10
  82.2 1.1 multiply_convert_fusion.1
  83.5 4.6 collective-permute-start.13
  88.2 0.8 collective-permute-done.13
  89.4 1.9 collective-permute-start.15
  91.3 3.4 collective-permute-start.14
  94.7 0.7 collective-permute-done.15
  95.5 4.0 collective-permute-done.14
  101.6 0.5 copy-done.3
  103.0 0.9 fusion.22
  104.2 3.4 collective-permute-start.16
  107.5 1.7 collective-permute-start.17
  109.9 1.9 collective-permute-start.19
  111.9 3.4 collective-permute-start.18
  115.4 3.8 collective-permute-done.18
  119.7 0.4 scatter-add.59
  120.1 1.4 fusion.119
  123.0 1.2 collective-permute-start.20
  124.2 2.9 collective-permute-start.21
  127.5 1.9 collective-permute-start.23
  129.4 3.4 collective-permute-start.22
  132.9 3.8 collective-permute-done.22
  137.2 0.4 scatter-add.65
  137.6 1.4 fusion.117
  140.6 4.1 collective-permute-start.25
  145.0 1.9 collective-permute-start.27
  147.0 3.4 collective-permute-start.26
  150.4 3.8 collective-permute-done.26
  154.8 0.6 scatter-add.71
  157.3 4.1 collective-permute-start.29
  161.7 1.9 collective-permute-start.31
  163.6 3.4 collective-permute-start.30
  167.0 97.9 %psum.23 = f32[512]{0:T(512)S(1)} all-reduce(f32[512]{0:T(512)S(1)} %add_add_fusion), channel_id=1, replica_groups=mesh['rep'=2,'ty'=16,'tx'=16] {'rep','ty','tx'}, use_global_device_ids=true, to_apply=%region_6.7 | all-reduce | flops 512 | bytes 4096 | tf_op jit(solution)/shard_map/psum | solution.py:142
  265.0 0.6 broadcast_multiply_fusion.2
  265.6 0.8 fusion.14
  266.4 0.8 fusion.17
  267.9 0.4 scatter-add.79
  268.3 0.6 add_bitcast_fusion
  268.9 259.4 %all-reduce.19.cloned.1.call-done = (f32[80,512]{1,0:T(8,128)}, f32[512,80]{0,1:T(8,128)}) async-done(((f32[80,512]{1,0:T(8,128)}, f32[512,80]{0,1:T(8,128)}), (f32[80,512]{1,0:T(8,128)}, f32[512,80]{0,1:T(8,128)})) %all-reduce.19.cloned.1.call-update) | async-done | bytes 327696 | tf_op jit(solution)/shard_map/psum | solution.py:142
  528.4 1.6 broadcast_multiply_fusion.1
  530.0 0.7 broadcast_multiply_fusion
  (315 shorter events, 19.7 us)
Async XLA Ops:
  7.2 33.1 %copy-start = (bf16[80,512]{1,0:T(8,128)(2,1)S(1)}, bf16[80,512]{1,0:T(8,128)(2,1)}, u32[]{:S(2)}) copy-start(bf16[80,512]{1,0:T(8,128)(2,1)} %param.46) | copy-start | bytes 245764
  7.2 8.4 %copy-start.1 = (f32[1,2,80,128]{3,2,1,0:T(8,128)S(1)}, f32[1,2,80,128]{3,2,1,0:T(8,128)}, u32[]{:S(2)}) copy-start(f32[1,2,80,128]{3,2,1,0:T(8,128)} %param.41) | copy-start | bytes 245764
  7.2 521.2 %all-reduce.19.cloned.1.call-start = ((), (), s32[]{:S(2)}) async-start(), calls=%async_computation | async-start | bytes 655360 | tf_op jit(solution)/shard_map/psum | solution.py:142
  8.1 6.9 %copy-start.6 = (s32[1,1,4]{2,1,0:T(1,128)S(1)}, s32[1,1,4]{2,1,0:T(1,128)}, u32[]{:S(2)}) copy-start(s32[1,1,4]{2,1,0:T(1,128)} %param.44) | copy-start | bytes 52
  8.1 18.8 %collective-permute-start = (f32[1,1,80,128]{3,2,1,0:T(8,128)S(1)}, f32[1,1,80,128]{3,2,1,0:T(8,128)S(1)}, u32[]{:S(2)}, u32[]{:S(2)}) collective-permute-start(f32[1,1,80,128]{3,2,1,0:T(8,128)S(1)} %get-tuple-element.309), channel_id=1, source_target_pairs={{0,16},{16,32},{32,48},{48,64},{64,80},{80,96},{96,112},{112,128},... | collective-permute-start | bytes 122888 | tf_op jit(solution)/shard_map/ppermute | solution.py:19
  11.6 15.3 %collective-permute-start.1 = (f32[1,1,80,128]{3,2,1,0:T(8,128)S(1)}, f32[1,1,80,128]{3,2,1,0:T(8,128)S(1)}, u32[]{:S(2)}, u32[]{:S(2)}) collective-permute-start(f32[1,1,80,128]{3,2,1,0:T(8,128)S(1)} %get-tuple-element.310), channel_id=1, source_target_pairs={{16,0},{32,16},{48,32},{64,48},{80,64},{96,80},{112,96},{128,112},... | collective-permute-start | bytes 122888 | tf_op jit(solution)/shard_map/ppermute | solution.py:20
  15.6 0.7 copy-start.7
  27.1 6.1 %collective-permute-start.3 = (f32[1,4,80,1]{3,2,1,0:T(8,128)S(1)}, f32[1,4,80,1]{3,2,1,0:T(8,128)S(1)}, u32[]{:S(2)}, u32[]{:S(2)}) collective-permute-start(f32[1,4,80,1]{3,2,1,0:T(8,128)S(1)} %get-tuple-element.238), channel_id=1, source_target_pairs={{1,0},{2,1},{3,2},{4,3},{5,4},{6,5},{7,6},{8,7},{9,8},{10,9},{11,1... | collective-permute-start | bytes 3848 | tf_op jit(solution)/shard_map/ppermute | solution.py:20
  29.7 8.2 %collective-permute-start.2 = (f32[1,4,80,1]{3,2,1,0:T(8,128)S(1)}, f32[1,4,80,1]{3,2,1,0:T(8,128)S(1)}, u32[]{:S(2)}, u32[]{:S(2)}) collective-permute-start(f32[1,4,80,1]{3,2,1,0:T(8,128)S(1)} %get-tuple-element.237), channel_id=1, source_target_pairs={{0,1},{1,2},{2,3},{3,4},{4,5},{5,6},{6,7},{7,8},{8,9},{9,10},{10,1... | collective-permute-start | bytes 3848 | tf_op jit(solution)/shard_map/ppermute | solution.py:19
  39.4 0.7 copy-start.5
  40.1 0.7 copy-start.8
  40.8 0.9 copy-start.2
  41.9 8.8 %collective-permute-start.5 = (f32[1,1,80,128]{3,2,1,0:T(8,128)S(1)}, f32[1,1,80,128]{3,2,1,0:T(8,128)S(1)}, u32[]{:S(2)}, u32[]{:S(2)}) collective-permute-start(f32[1,1,80,128]{3,2,1,0:T(8,128)S(1)} %get-tuple-element.304), channel_id=1, source_target_pairs={{16,0},{32,16},{48,32},{64,48},{80,64},{96,80},{112,96},{128,112},... | collective-permute-start | bytes 122888 | tf_op jit(solution)/shard_map/ppermute | solution.py:20
  49.9 1.2 collective-permute-start.4
  51.2 6.1 %collective-permute-start.7 = (f32[1,4,80,1]{3,2,1,0:T(8,128)S(1)}, f32[1,4,80,1]{3,2,1,0:T(8,128)S(1)}, u32[]{:S(2)}, u32[]{:S(2)}) collective-permute-start(f32[1,4,80,1]{3,2,1,0:T(8,128)S(1)} %get-tuple-element.236), channel_id=1, source_target_pairs={{1,0},{2,1},{3,2},{4,3},{5,4},{6,5},{7,6},{8,7},{9,8},{10,9},{11,1... | collective-permute-start | bytes 3848 | tf_op jit(solution)/shard_map/ppermute | solution.py:20
  53.1 8.2 %collective-permute-start.6 = (f32[1,4,80,1]{3,2,1,0:T(8,128)S(1)}, f32[1,4,80,1]{3,2,1,0:T(8,128)S(1)}, u32[]{:S(2)}, u32[]{:S(2)}) collective-permute-start(f32[1,4,80,1]{3,2,1,0:T(8,128)S(1)} %get-tuple-element.235), channel_id=1, source_target_pairs={{0,1},{1,2},{2,3},{3,4},{4,5},{5,6},{6,7},{7,8},{8,9},{9,10},{10,1... | collective-permute-start | bytes 3848 | tf_op jit(solution)/shard_map/ppermute | solution.py:19
  64.4 5.5 %collective-permute-start.9 = (f32[1,1,80,128]{3,2,1,0:T(8,128)S(1)}, f32[1,1,80,128]{3,2,1,0:T(8,128)S(1)}, u32[]{:S(2)}, u32[]{:S(2)}) collective-permute-start(f32[1,1,80,128]{3,2,1,0:T(8,128)S(1)} %get-tuple-element.298), channel_id=1, source_target_pairs={{16,0},{32,16},{48,32},{64,48},{80,64},{96,80},{112,96},{128,112},... | collective-permute-start | bytes 122888 | tf_op jit(solution)/shard_map/ppermute | solution.py:20
  69.0 1.2 collective-permute-start.8
  70.3 6.1 %collective-permute-start.11 = (f32[1,4,80,1]{3,2,1,0:T(8,128)S(1)}, f32[1,4,80,1]{3,2,1,0:T(8,128)S(1)}, u32[]{:S(2)}, u32[]{:S(2)}) collective-permute-start(f32[1,4,80,1]{3,2,1,0:T(8,128)S(1)} %get-tuple-element.234), channel_id=1, source_target_pairs={{1,0},{2,1},{3,2},{4,3},{5,4},{6,5},{7,6},{8,7},{9,8},{10,9},{11,1... | collective-permute-start | bytes 3848 | tf_op jit(solution)/shard_map/ppermute | solution.py:20
  72.2 8.2 %collective-permute-start.10 = (f32[1,4,80,1]{3,2,1,0:T(8,128)S(1)}, f32[1,4,80,1]{3,2,1,0:T(8,128)S(1)}, u32[]{:S(2)}, u32[]{:S(2)}) collective-permute-start(f32[1,4,80,1]{3,2,1,0:T(8,128)S(1)} %get-tuple-element.233), channel_id=1, source_target_pairs={{0,1},{1,2},{2,3},{3,4},{4,5},{5,6},{6,7},{7,8},{8,9},{9,10},{10,1... | collective-permute-start | bytes 3848 | tf_op jit(solution)/shard_map/ppermute | solution.py:19
  83.5 5.5 %collective-permute-start.13 = (f32[1,1,80,128]{3,2,1,0:T(8,128)S(1)}, f32[1,1,80,128]{3,2,1,0:T(8,128)S(1)}, u32[]{:S(2)}, u32[]{:S(2)}) collective-permute-start(f32[1,1,80,128]{3,2,1,0:T(8,128)S(1)} %get-tuple-element.292), channel_id=1, source_target_pairs={{16,0},{32,16},{48,32},{64,48},{80,64},{96,80},{112,96},{128,112},... | collective-permute-start | bytes 122888 | tf_op jit(solution)/shard_map/ppermute | solution.py:20
  88.1 1.2 collective-permute-start.12
  89.4 6.1 %collective-permute-start.15 = (f32[1,4,80,1]{3,2,1,0:T(8,128)S(1)}, f32[1,4,80,1]{3,2,1,0:T(8,128)S(1)}, u32[]{:S(2)}, u32[]{:S(2)}) collective-permute-start(f32[1,4,80,1]{3,2,1,0:T(8,128)S(1)} %get-tuple-element.232), channel_id=1, source_target_pairs={{1,0},{2,1},{3,2},{4,3},{5,4},{6,5},{7,6},{8,7},{9,8},{10,9},{11,1... | collective-permute-start | bytes 3848 | tf_op jit(solution)/shard_map/ppermute | solution.py:20
  91.3 8.2 %collective-permute-start.14 = (f32[1,4,80,1]{3,2,1,0:T(8,128)S(1)}, f32[1,4,80,1]{3,2,1,0:T(8,128)S(1)}, u32[]{:S(2)}, u32[]{:S(2)}) collective-permute-start(f32[1,4,80,1]{3,2,1,0:T(8,128)S(1)} %get-tuple-element.231), channel_id=1, source_target_pairs={{0,1},{1,2},{2,3},{3,4},{4,5},{5,6},{6,7},{7,8},{8,9},{9,10},{10,1... | collective-permute-start | bytes 3848 | tf_op jit(solution)/shard_map/ppermute | solution.py:19
  101.3 0.9 copy-start.3
  104.2 15.1 %collective-permute-start.16 = (f32[1,1,80,128]{3,2,1,0:T(8,128)S(1)}, f32[1,1,80,128]{3,2,1,0:T(8,128)S(1)}, u32[]{:S(2)}, u32[]{:S(2)}) collective-permute-start(f32[1,1,80,128]{3,2,1,0:T(8,128)S(1)} %get-tuple-element.278), channel_id=1, source_target_pairs={{0,16},{16,32},{32,48},{48,64},{64,80},{80,96},{96,112},{112,128},... | collective-permute-start | bytes 122888 | tf_op jit(solution)/shard_map/ppermute | solution.py:19
  107.5 11.8 %collective-permute-start.17 = (f32[1,1,80,128]{3,2,1,0:T(8,128)S(1)}, f32[1,1,80,128]{3,2,1,0:T(8,128)S(1)}, u32[]{:S(2)}, u32[]{:S(2)}) collective-permute-start(f32[1,1,80,128]{3,2,1,0:T(8,128)S(1)} %get-tuple-element.277), channel_id=1, source_target_pairs={{16,0},{32,16},{48,32},{64,48},{80,64},{96,80},{112,96},{128,112},... | collective-permute-start | bytes 122888 | tf_op jit(solution)/shard_map/ppermute | solution.py:20
  109.9 5.4 %collective-permute-start.19 = (f32[1,2,80,1]{3,2,1,0:T(8,128)S(1)}, f32[1,2,80,1]{3,2,1,0:T(8,128)S(1)}, u32[]{:S(2)}, u32[]{:S(2)}) collective-permute-start(f32[1,2,80,1]{3,2,1,0:T(8,128)S(1)} %get-tuple-element.276), channel_id=1, source_target_pairs={{1,0},{2,1},{3,2},{4,3},{5,4},{6,5},{7,6},{8,7},{9,8},{10,9},{11,1... | collective-permute-start | bytes 1928 | tf_op jit(solution)/shard_map/ppermute | solution.py:20
  111.9 7.3 %collective-permute-start.18 = (f32[1,2,80,1]{3,2,1,0:T(8,128)S(1)}, f32[1,2,80,1]{3,2,1,0:T(8,128)S(1)}, u32[]{:S(2)}, u32[]{:S(2)}) collective-permute-start(f32[1,2,80,1]{3,2,1,0:T(8,128)S(1)} %get-tuple-element.275), channel_id=1, source_target_pairs={{0,1},{1,2},{2,3},{3,4},{4,5},{5,6},{6,7},{7,8},{8,9},{9,10},{10,1... | collective-permute-start | bytes 1928 | tf_op jit(solution)/shard_map/ppermute | solution.py:19
  123.0 13.8 %collective-permute-start.20 = (f32[1,1,80,128]{3,2,1,0:T(8,128)S(1)}, f32[1,1,80,128]{3,2,1,0:T(8,128)S(1)}, u32[]{:S(2)}, u32[]{:S(2)}) collective-permute-start(f32[1,1,80,128]{3,2,1,0:T(8,128)S(1)} %get-tuple-element.266), channel_id=1, source_target_pairs={{0,16},{16,32},{32,48},{48,64},{64,80},{80,96},{96,112},{112,128},... | collective-permute-start | bytes 122888 | tf_op jit(solution)/shard_map/ppermute | solution.py:19
  124.2 12.6 %collective-permute-start.21 = (f32[1,1,80,128]{3,2,1,0:T(8,128)S(1)}, f32[1,1,80,128]{3,2,1,0:T(8,128)S(1)}, u32[]{:S(2)}, u32[]{:S(2)}) collective-permute-start(f32[1,1,80,128]{3,2,1,0:T(8,128)S(1)} %get-tuple-element.265), channel_id=1, source_target_pairs={{16,0},{32,16},{48,32},{64,48},{80,64},{96,80},{112,96},{128,112},... | collective-permute-start | bytes 122888 | tf_op jit(solution)/shard_map/ppermute | solution.py:20
  127.5 5.4 %collective-permute-start.23 = (f32[1,2,80,1]{3,2,1,0:T(8,128)S(1)}, f32[1,2,80,1]{3,2,1,0:T(8,128)S(1)}, u32[]{:S(2)}, u32[]{:S(2)}) collective-permute-start(f32[1,2,80,1]{3,2,1,0:T(8,128)S(1)} %get-tuple-element.264), channel_id=1, source_target_pairs={{1,0},{2,1},{3,2},{4,3},{5,4},{6,5},{7,6},{8,7},{9,8},{10,9},{11,1... | collective-permute-start | bytes 1928 | tf_op jit(solution)/shard_map/ppermute | solution.py:20
  129.4 7.3 %collective-permute-start.22 = (f32[1,2,80,1]{3,2,1,0:T(8,128)S(1)}, f32[1,2,80,1]{3,2,1,0:T(8,128)S(1)}, u32[]{:S(2)}, u32[]{:S(2)}) collective-permute-start(f32[1,2,80,1]{3,2,1,0:T(8,128)S(1)} %get-tuple-element.263), channel_id=1, source_target_pairs={{0,1},{1,2},{2,3},{3,4},{4,5},{5,6},{6,7},{7,8},{8,9},{9,10},{10,1... | collective-permute-start | bytes 1928 | tf_op jit(solution)/shard_map/ppermute | solution.py:19
  140.5 13.8 %collective-permute-start.24 = (f32[1,1,80,128]{3,2,1,0:T(8,128)S(1)}, f32[1,1,80,128]{3,2,1,0:T(8,128)S(1)}, u32[]{:S(2)}, u32[]{:S(2)}) collective-permute-start(f32[1,1,80,128]{3,2,1,0:T(8,128)S(1)} %get-tuple-element.254), channel_id=1, source_target_pairs={{0,16},{16,32},{32,48},{48,64},{64,80},{80,96},{96,112},{112,128},... | collective-permute-start | bytes 122888 | tf_op jit(solution)/shard_map/ppermute | solution.py:19
  140.6 13.8 %collective-permute-start.25 = (f32[1,1,80,128]{3,2,1,0:T(8,128)S(1)}, f32[1,1,80,128]{3,2,1,0:T(8,128)S(1)}, u32[]{:S(2)}, u32[]{:S(2)}) collective-permute-start(f32[1,1,80,128]{3,2,1,0:T(8,128)S(1)} %get-tuple-element.253), channel_id=1, source_target_pairs={{16,0},{32,16},{48,32},{64,48},{80,64},{96,80},{112,96},{128,112},... | collective-permute-start | bytes 122888 | tf_op jit(solution)/shard_map/ppermute | solution.py:20
  145.0 5.4 %collective-permute-start.27 = (f32[1,2,80,1]{3,2,1,0:T(8,128)S(1)}, f32[1,2,80,1]{3,2,1,0:T(8,128)S(1)}, u32[]{:S(2)}, u32[]{:S(2)}) collective-permute-start(f32[1,2,80,1]{3,2,1,0:T(8,128)S(1)} %get-tuple-element.252), channel_id=1, source_target_pairs={{1,0},{2,1},{3,2},{4,3},{5,4},{6,5},{7,6},{8,7},{9,8},{10,9},{11,1... | collective-permute-start | bytes 1928 | tf_op jit(solution)/shard_map/ppermute | solution.py:20
  147.0 7.3 %collective-permute-start.26 = (f32[1,2,80,1]{3,2,1,0:T(8,128)S(1)}, f32[1,2,80,1]{3,2,1,0:T(8,128)S(1)}, u32[]{:S(2)}, u32[]{:S(2)}) collective-permute-start(f32[1,2,80,1]{3,2,1,0:T(8,128)S(1)} %get-tuple-element.251), channel_id=1, source_target_pairs={{0,1},{1,2},{2,3},{3,4},{4,5},{5,6},{6,7},{7,8},{8,9},{9,10},{10,1... | collective-permute-start | bytes 1928 | tf_op jit(solution)/shard_map/ppermute | solution.py:19
  157.2 110.3 %collective-permute-start.28 = (f32[1,1,80,128]{3,2,1,0:T(8,128)S(1)}, f32[1,1,80,128]{3,2,1,0:T(8,128)S(1)}, u32[]{:S(2)}, u32[]{:S(2)}) collective-permute-start(f32[1,1,80,128]{3,2,1,0:T(8,128)S(1)} %get-tuple-element.242), channel_id=1, source_target_pairs={{0,16},{16,32},{32,48},{48,64},{64,80},{80,96},{96,112},{112,128},... | collective-permute-start | bytes 122888 | tf_op jit(solution)/shard_map/ppermute | solution.py:19
  157.3 110.3 %collective-permute-start.29 = (f32[1,1,80,128]{3,2,1,0:T(8,128)S(1)}, f32[1,1,80,128]{3,2,1,0:T(8,128)S(1)}, u32[]{:S(2)}, u32[]{:S(2)}) collective-permute-start(f32[1,1,80,128]{3,2,1,0:T(8,128)S(1)} %get-tuple-element.241), channel_id=1, source_target_pairs={{16,0},{32,16},{48,32},{64,48},{80,64},{96,80},{112,96},{128,112},... | collective-permute-start | bytes 122888 | tf_op jit(solution)/shard_map/ppermute | solution.py:20
  161.7 105.7 %collective-permute-start.31 = (f32[1,2,80,1]{3,2,1,0:T(8,128)S(1)}, f32[1,2,80,1]{3,2,1,0:T(8,128)S(1)}, u32[]{:S(2)}, u32[]{:S(2)}) collective-permute-start(f32[1,2,80,1]{3,2,1,0:T(8,128)S(1)} %get-tuple-element.240), channel_id=1, source_target_pairs={{1,0},{2,1},{3,2},{4,3},{5,4},{6,5},{7,6},{8,7},{9,8},{10,9},{11,1... | collective-permute-start | bytes 1928 | tf_op jit(solution)/shard_map/ppermute | solution.py:20
  163.6 103.7 %collective-permute-start.30 = (f32[1,2,80,1]{3,2,1,0:T(8,128)S(1)}, f32[1,2,80,1]{3,2,1,0:T(8,128)S(1)}, u32[]{:S(2)}, u32[]{:S(2)}) collective-permute-start(f32[1,2,80,1]{3,2,1,0:T(8,128)S(1)} %get-tuple-element.239), channel_id=1, source_target_pairs={{0,1},{1,2},{2,3},{3,4},{4,5},{5,6},{6,7},{7,8},{8,9},{9,10},{10,1... | collective-permute-start | bytes 1928 | tf_op jit(solution)/shard_map/ppermute | solution.py:19
  528.4 1.6 copy-start.4
Sparse Core Ops, SparseCore 0:
  267.4 260.9 all-reduce.18
where the time goes:
time: 540 us; the launch traced here: 538 us
  waiting for transfers between devices  294 us (54%)
  blocking collectives  97.9 us (18%)
  starting transfers between devices  83.8 us (16%)
  between operations  26.8 us (5%)
  local copies, waits for them, and re-layouts  14.1 us (3%)
  matrix products  11.4 us (2%)
  other arithmetic  9.5 us (2%)
    psum x1, waiting for transfers between devices, shards(): lax.psum((total_in, total_out, total_bias), ('rep', 'ty', 'tx'))  259 us
    psum x1, blocking collectives, shards(): lax.psum((total_in, total_out, total_bias), ('rep', 'ty', 'tx'))  97.9 us
    ppermute x16, starting transfers between devices, extended(): after = lax.ppermute(first, axis, down)  49.4 us
    ppermute x16, starting transfers between devices, extended(): before = lax.ppermute(last, axis, up)  34.4 us
    ppermute x16, waiting for transfers between devices, extended(): before = lax.ppermute(last, axis, up)  29.3 us
  transfers between devices with their start and end apart: 33, of which 18 were waited for; matrix products, arithmetic and copies ran while one was open for 1% of the time, Pallas kernels for 0%

commit v1 on v0

v1 whole, which is shorter than its diff:
```python
import functools
import math

import jax
import jax.numpy as jnp
from jax import lax
from jax.experimental import pallas as pl
from jax.experimental.pallas import tpu as pltpu
from jax.sharding import PartitionSpec as P

LEV = 16
SUBSTEPS = 4
C = 80
X = 128
HID = 512
KA = 96
RED = 96
PIECE = 16
OWNERS = RED // PIECE
MESH = pl.DeviceIdType.MESH
F32 = jnp.float32
BF16 = jnp.bfloat16


def places():
    r, t, c = lax.axis_index("rep"), lax.axis_index("ty"), lax.axis_index("tx")
    return r, t, c, t % 2, 2 * r + c // 8, c % 8, t // 2


def at_core():
    r, t, c, core, x, y, z = places()
    return (r, t + 1 - 2 * core, c)


def at_x(j):
    r, t, c, core, x, y, z = places()
    xx = (x + j) % 4
    return (xx // 2, t, (xx % 2) * 8 + y)


def at_y(j):
    r, t, c, core, x, y, z = places()
    return (r, t, (c // 8) * 8 + (y + j) % 8)


def at_z(j):
    r, t, c, core, x, y, z = places()
    return (r, ((z + j) % 8) * 2 + core, c)


def beside():
    r, t, c = places()[:3]
    return (
        (r, (t + 15) % 16, c),
        (r, (t + 1) % 16, c),
        (r, t, (c + 15) % 16),
        (r, t, (c + 1) % 16),
    )


def corners():
    r, t, c = places()[:3]
    return [(r, (t + dt) % 16, (c + dc) % 16) for dt in (15, 1) for dc in (15, 1)]


def remote(src, dst, send, recv, device):
    return pltpu.make_async_remote_copy(
        src_ref=src, dst_ref=dst, send_sem=send, recv_sem=recv, device_id=device, device_id_type=MESH
    )


def lanes(shape=(8, X)):
    return lax.broadcasted_iota(jnp.int32, shape, 1)


def flip_lanes(block):
    index = X - 1 - lanes(block.shape)
    return jnp.take_along_axis(block, index, axis=1, mode="promise_in_bounds")


def code_parts(seams, k):
    code = jnp.broadcast_to(seams[:, k : k + 1], (8, X))
    one = (code > 0.5) & (code < 1.5)
    two = (code > 1.5) & (code < 2.5)
    rev = jnp.where(one | two, 1.0, 0.0)
    cos = jnp.where(code < 0.5, 1.0, 0.0) - jnp.where(two, 1.0, 0.0)
    sin = jnp.where(one, 1.0, 0.0) - jnp.where(code > 2.5, 1.0, 0.0)
    return rev, cos, sin


def turn_row(row, parts, inverse):
    rev, cos, sin = parts
    if inverse:
        sin = -sin
    mask = rev > 0.5
    blocks = []
    for k in range(C // 8):
        block = row[8 * k : 8 * k + 8]
        blocks.append(jnp.where(mask, flip_lanes(block), block))
    u, v = blocks[0:2], blocks[2:4]
    new_u = [cos * a - sin * b for a, b in zip(u, v)]
    new_v = [sin * a + cos * b for a, b in zip(u, v)]
    return jnp.concatenate(new_u + new_v + blocks[4:], axis=0)


def pack(rows):
    lane = lanes()
    packed = jnp.zeros((8, X), F32)
    for y in range(2):
        for k in range(C // 8):
            place = 64 * y + 2 * k
            moved = pltpu.roll(rows[y][8 * k : 8 * k + 8], (place + 1) % X, 1)
            packed = jnp.where((lane == place) | (lane == place + 1), moved, packed)
    return packed


def swap_sides(from_west, from_east):
    odd = lanes() % 2 == 1
    return jnp.where(odd, pltpu.roll(from_west, 1, 1), pltpu.roll(from_east, X - 1, 1))


def turn_pack(packed, tables, inverse):
    return spin_pack(jnp.where(tables[0] > 0.5, pltpu.roll(packed, 64, 1), packed), tables, inverse)


def spin_pack(packed, tables, inverse):
    rev, cos, sin_u, sin_v = tables
    spin = sin_v * pltpu.roll(packed, 4, 1) - sin_u * pltpu.roll(packed, X - 4, 1)
    return cos * packed - spin if inverse else cos * packed + spin


def by_side(west, east):
    odd = lanes() % 2 == 1
    return [jnp.where(odd, w, e) for w, e in zip(west, east)]


def pack_tables(west, east):
    return spread_tables(*by_side(west, east))


def spread_tables(rev, cos, sin):
    lane = lanes()
    at = lane % 64
    zero = jnp.zeros((8, X), F32)
    cos = jnp.where(at < 8, cos, zero + 1.0)
    return rev, cos, jnp.where(at < 4, sin, zero), jnp.where((at >= 4) & (at < 8), sin, zero)


def seconds(rows):
    first = lanes((C, X)) == 0
    return [jnp.where(first, pltpu.roll(row, X - 1, 1), pltpu.roll(row, 1, 1)) for row in rows]


def ends_beyond(north_pack, south_pack, tables):
    lane = lanes()
    wests = jnp.where(lane >= 64, north_pack[0], south_pack[0])
    easts = jnp.where(lane >= 64, north_pack[1], south_pack[1])
    rev = tables[0] > 0.5
    at_west = jnp.where(rev, pltpu.roll(wests, 64, 1), pltpu.roll(wests, 65, 1))
    at_east = jnp.where(rev, pltpu.roll(easts, 64, 1), pltpu.roll(easts, 63, 1))
    valid = lane % 64 < 2 * (C // 8)
    picked = jnp.where(valid, jnp.where(lane % 2 == 1, at_west, at_east), 0.0)
    return spin_pack(picked, tables, False)


def ends_back(north_pack, south_pack):
    lane = lanes()
    wests = jnp.where(lane >= 64, north_pack[0], south_pack[0])
    easts = jnp.where(lane >= 64, north_pack[1], south_pack[1])
    picked = jnp.where(lane % 2 == 1, pltpu.roll(wests, 65, 1), pltpu.roll(easts, 63, 1))
    return jnp.where(lane % 64 < 2 * (C // 8), picked, 0.0)


def unfold(packed):
    return jnp.concatenate(
        [packed] + [pltpu.roll(packed, X - 2 * k, 1) for k in range(1, C // 8)], axis=0
    )


def fold(columns):
    at = lanes() % 64
    packed = jnp.where(at < 2, columns[:8], 0.0)
    for k in range(1, C // 8):
        moved = pltpu.roll(columns[8 * k : 8 * k + 8], 2 * k, 1)
        packed = jnp.where((at == 2 * k) | (at == 2 * k + 1), moved, packed)
    return packed


def edges(packed, y):
    lane = lanes()
    mask = (lane == 0) | (lane == X - 1)
    zero = jnp.zeros((8, X), F32)
    return jnp.concatenate(
        [
            jnp.where(mask, pltpu.roll(packed, (X - (64 * y + 2 * k + 1)) % X, 1), zero)
            for k in range(C // 8)
        ],
        axis=0,
    )


def inner_row(row, other):
    lane = lanes((C, X))
    left = jnp.where(lane == 0, 0.0, pltpu.roll(row, 1, 1))
    right = jnp.where(lane == X - 1, 0.0, pltpu.roll(row, X - 1, 1))
    return left + right + other - 4.0 * row


def inner(rows):
    return [inner_row(rows[0], rows[1]), inner_row(rows[1], rows[0])]


def dot(a, b, dims=((1,), (0,))):
    return lax.dot_general(a, b, (dims, ((), ())), preferred_element_type=F32)


def step_kernel(
    factor,
    *refs,
):
    operands, (final_ref, grad_ref, sums_ref), loaded, refs = refs[:9], refs[9:12], refs[12:21], refs[21:]
    face_ref, seam_ref, state_ref, cot_ref, kappa_ref, rate_ref, w_in_ref, bias_ref, w_out_t = loaded
    (
    load_sem, w_in_t, w_out_ref, coef_ref, inputs_ref, hidden_ref, slope_ref, bias_acc, acc_in, acc_out,
    row_out, col_out, row_in, col_in,
    tile_out, pair_out, tile_in, pair_in, corner_in, note_out, note_in, back_out, turned_out, turned_in, outer_slope,
    mine, half_in, x_in, tile_ref, y_in, piece_ref, z_in, all_ref, final_vmem, grad_vmem,
    row_send, row_recv, col_send, col_recv, deep_send, deep_recv, note_send, note_recv,
    core_send, core_recv, xs_send, xs_recv, ys_send, ys_recv, zs_send, zs_recv,
    yg_send, yg_recv, xg_send, xg_recv, cg_send, cg_recv, keep_sem, result_sem,
    ) = refs
    rep, ty, tx, core, x, y, z = places()
    north, south, west, east = beside()
    barrier = pltpu.get_barrier_semaphore()
    friends = [north, south, west, east] + corners() + [at_x(j) for j in range(1, 4)]
    friends += [at_y(3), at_y(5), at_z(2), at_z(6)]
    for friend in friends:
        pl.semaphore_signal(barrier, inc=1, device_id=friend, device_id_type=MESH)

    loads = [
        pltpu.make_async_copy(operand, ref, load_sem.at[n])
        for n, (operand, ref) in enumerate(zip(operands, loaded))
    ]
    for n in (2, 0, 1, 4, 5, 6, 7, 8, 3):
        loads[n].start()
    results = [
        pltpu.make_async_copy(final_vmem, final_ref.at[0], result_sem.at[0]),
        pltpu.make_async_copy(grad_vmem, grad_ref.at[0], result_sem.at[1]),
    ]
    copies = []

    def start(copy):
        copy.start()
        copies.append(copy)
        return copy

    def exchange(e, first, last):
        return [
            start(remote(col_out.at[e], col_in.at[e, 1], col_send.at[e, 0], col_recv.at[e, 1], west)),
            start(remote(col_out.at[e], col_in.at[e, 0], col_send.at[e, 1], col_recv.at[e, 0], east)),
            start(remote(first, row_in.at[e, 1], row_send.at[e, 0], row_recv.at[e, 1], north)),
            start(remote(last, row_in.at[e, 0], row_send.at[e, 1], row_recv.at[e, 0], south)),
        ]

    def arrived(flights):
        for flight in flights:
            flight.wait_recv()

    def deep_tiles(d, tiles):
        return [
            start(remote(tiles[n], tile_in.at[d, 1 - n], deep_send.at[d, n], deep_recv.at[d, 1 - n], device))
            for n, device in enumerate((north, south))
        ]

    def deep_corners(d, corner_out, corner_in):
        return [
            start(remote(corner_out, corner_in.at[3 - n], deep_send.at[d, 4 + n], deep_recv.at[d, 7 - n], device))
            for n, device in enumerate(corners())
        ]

    def deep_sides(d):
        return [
            start(remote(pair_out.at[d], pair_in.at[d, 1 - n], deep_send.at[d, 2 + n], deep_recv.at[d, 3 - n], device))
            for n, device in enumerate((west, east))
        ]

    loads[2].wait()
    field = [state_ref[0, 0], state_ref[0, 1]]
    pair_out[0, 0] = pack(field)
    pair_out[0, 1] = pack(seconds(field))
    pl.semaphore_wait(barrier, len(friends))
    flights = deep_corners(0, pair_out.at[0, 0], corner_in.at[0])
    flights += deep_tiles(0, [state_ref.at[0]] * 2) + deep_sides(0)

    for n in (0, 1, 4, 5, 6, 7, 8):
        loads[n].wait()
    seams = seam_ref[0].astype(F32)
    parts = [code_parts(seams, k) for k in range(4)]
    tables = pack_tables(parts[2], parts[3])
    rate_row = jnp.zeros((1, C), F32)
    face_here = jnp.broadcast_to(face_ref[...], (1, C))
    for face in range(rate_ref.shape[0]):
        rate_row = rate_row + jnp.where(face_here == face, 1.0, 0.0) * rate_ref[face : face + 1, :]
    rate = jnp.broadcast_to(rate_row, (X, C)).T
    coefs = [rate * kappa_ref[k : k + 1, :] for k in range(2)]
    for k in range(2):
        coef_ref[k] = coefs[k]
    note_out[0] = jnp.zeros((8, X), F32)
    note_out[0, 0:2] = kappa_ref[...]
    note_out[0, 2:3, 0:C] = rate_row
    note_out[0, 3:4, 0:4] = seams
    note_out[1] = pack(coefs)
    flights += [
        start(remote(note_out, note_in.at[n ^ 1], note_send.at[n], note_recv.at[n ^ 1], device))
        for n, device in enumerate((north, south, west, east))
    ]
    bias = bias_ref[...]
    high = bias.astype(BF16).astype(F32)
    middle = (bias - high).astype(BF16).astype(F32)
    low = bias - high - middle
    at_row = lax.broadcasted_iota(jnp.int32, (KA - C, HID), 0)
    extra = jnp.where(at_row == 0, high, jnp.where(at_row == 1, middle, jnp.where(at_row == 2, low, 0.0)))
    w_in_t[...] = jnp.concatenate([w_in_ref[...].astype(F32), extra], axis=0).T.astype(BF16)
    w_out_ref[...] = w_out_t[...].astype(F32).T.astype(BF16)
    ones = jnp.where(lax.broadcasted_iota(jnp.int32, (KA - C, 2 * X), 0) < 3, 1.0, 0.0).astype(BF16)

    def network(s, inputs, slope_at):
        width = inputs.shape[1]
        filler = jnp.concatenate([ones] * (-(-width // (2 * X))), axis=1)[:, :width]
        z_all = dot(w_in_t[...], jnp.concatenate([inputs, filler], axis=0))
        squashed = 0.5 + 0.5 * jnp.tanh(0.5 * z_all)
        silu = z_all * squashed
        hidden = silu.astype(BF16)
        if s is not None:
            inputs_ref[s] = inputs
            hidden_ref[s] = hidden
        if slope_at is not None:
            slope_at[...] = squashed + silu * (1.0 - squashed)
        return dot(w_out_t[...], hidden)

    def own_step(s, field, inside, above, below, sides):
        rims = turn_pack(sides, tables, False)
        pre = []
        for k, beyond in enumerate((above, below)):
            rim = turn_row(beyond, parts[k], False)
            pre.append(field[k] + coef_ref[k] * (inside[k] + rim + edges(rims, k)))
        added = network(s, jnp.concatenate(pre, axis=1).astype(BF16), slope_ref.at[s])
        return [pre[k] + added[:, X * k : X * k + X] for k in range(2)]

    for d in range(SUBSTEPS // 2):
        inside = inner(field)
        arrived(flights)
        if d == 0:
            codes = [[code_parts(note_in[n, 0, 3:4, 0:4], k) for k in range(4)] for n in range(4)]
            of_north, of_south, of_west, of_east = codes
            north_tables = pack_tables(of_north[2], of_north[3])
            south_tables = pack_tables(of_south[2], of_south[3])
            back_tables = pack_tables(of_west[3], of_east[2])
            upper = lanes() < 64
            end_tables = spread_tables(*[
                jnp.where(upper, a, b)
                for a, b in zip(by_side(of_west[0], of_east[0]), by_side(of_west[1], of_east[1]))
            ])
            far_coef = [
                jnp.broadcast_to(note_in[n, 0, 2:3], (X, X)).T[:C] * note_in[n, 0, 1 - n : 2 - n]
                for n in range(2)
            ]
            row_tables = spread_tables(*[jnp.where(upper, a, b) for a, b in zip(parts[0], parts[1])])
            side_coef = swap_sides(note_in[2, 1], note_in[3, 1])
        sides = swap_sides(pair_in[d, 0, 0], pair_in[d, 1, 0])
        nearer = swap_sides(pair_in[d, 0, 1], pair_in[d, 1, 1])
        up, down = tile_in[d, 0, 1], tile_in[d, 1, 0]
        up_sides = turn_pack(swap_sides(corner_in[d, 0], corner_in[d, 1]), north_tables, False)
        down_sides = turn_pack(swap_sides(corner_in[d, 2], corner_in[d, 3]), south_tables, False)
        up_pre = up + far_coef[0] * (
            inner_row(up, tile_in[d, 0, 0]) + turn_row(field[0], of_north[1], False) + edges(up_sides, 1)
        )
        down_pre = down + far_coef[1] * (
            inner_row(down, tile_in[d, 1, 1]) + turn_row(field[1], of_south[0], False) + edges(down_sides, 0)
        )
        ends = ends_beyond(
            (corner_in[d, 0], corner_in[d, 1]), (corner_in[d, 2], corner_in[d, 3]), end_tables
        )
        sides_pre = sides + side_coef * (
            nearer + turn_pack(pair_out[d, 0], back_tables, False) + pltpu.roll(sides, 64, 1) + ends - 4.0 * sides
        )
        field = own_step(2 * d, field, inside, up, down, sides)
        outer = jnp.concatenate([up_pre, down_pre, unfold(sides_pre)], axis=1).astype(BF16)
        added = network(None, outer, None if 2 * d + 2 < SUBSTEPS else outer_slope)
        up = up_pre + added[:, :X]
        down = down_pre + added[:, X : 2 * X]
        sides = sides_pre + fold(added[:, 2 * X :])
        field = own_step(2 * d + 1, field, inner(field), up, down, sides)
        if 2 * d + 2 < SUBSTEPS:
            pair_out[d + 1, 0] = pack(field)
            flights = deep_corners(d + 1, pair_out.at[d + 1, 0], corner_in.at[d + 1])
            for k in range(2):
                tile_out[k] = field[k]
            flights += deep_tiles(d + 1, [tile_out] * 2)
            pair_out[d + 1, 1] = pack(seconds(field))
            flights += deep_sides(d + 1)
        else:
            for k in range(2):
                final_vmem[k] = field[k]
            results[0].start()

    loads[3].wait()
    def network_back(cot_b, slope):
        gate = dot(w_out_ref[...], cot_b) * slope
        gate_b = gate.astype(BF16)
        return gate, gate_b, dot(w_in_ref[...], gate_b)

    def own_back(s, grad):
        cot_b = jnp.concatenate(grad, axis=1).astype(BF16)
        gate, gate_b, back = network_back(cot_b, slope_ref[s])
        return [grad[k] + back[:, X * k : X * k + X] for k in range(2)], (s, cot_b, gate, gate_b)

    def gather(known):
        s, cot_b, gate, gate_b = known
        folded = gate[:, :X] + gate[:, X:]
        dw_in = dot(inputs_ref[s], gate_b, ((1,), (1,)))
        dw_out = dot(cot_b, hidden_ref[s], ((1,), (1,)))
        if s < SUBSTEPS - 1:
            folded = folded + bias_acc[...]
            dw_in = dw_in + acc_in[...]
            dw_out = dw_out + acc_out[...]
        if s > 0:
            bias_acc[...] = folded
            acc_in[...] = dw_in
            acc_out[...] = dw_out
        return folded, dw_in, dw_out

    pre_grad, known = own_back(SUBSTEPS - 1, [cot_ref[0, 0], cot_ref[0, 1]])
    weighted = [coef_ref[k] * pre_grad[k] for k in range(2)]
    packed = pack(pre_grad)
    weighted_pack = note_out[1] * packed
    own_turned = turn_pack(weighted_pack, tables, True)
    turned_out[0] = own_turned
    turned_out[1] = spin_pack(
        jnp.where(row_tables[0] > 0.5, swap_sides(weighted_pack, weighted_pack), weighted_pack), row_tables, True
    )
    flights = deep_corners(2, turned_out, turned_in)
    back_out[0, 0], back_out[0, 1] = pre_grad[0], weighted[1]
    back_out[1, 0], back_out[1, 1] = weighted[0], pre_grad[1]
    flights += deep_tiles(2, [back_out.at[0], back_out.at[1]])
    pair_out[2, 0] = packed
    pair_out[2, 1] = pack(seconds(weighted))
    flights += deep_sides(2)
    gather(known)
    inside = inner(weighted)
    to_north, to_south = [turn_row(weighted[k], parts[k], True) for k in range(2)]
    arrived(flights)
    up, down = tile_in[2, 0, 1], tile_in[2, 1, 0]
    sides = swap_sides(pair_in[2, 0, 0], pair_in[2, 1, 0])
    nearer = swap_sides(pair_in[2, 0, 1], pair_in[2, 1, 1])
    up_w, down_w, sides_w = far_coef[0] * up, far_coef[1] * down, side_coef * sides

    def spread_back(pre_grad, inside, up_w, down_w, sides_w):
        rims = turn_pack(sides_w, back_tables, True)
        beyond = [turn_row(up_w, of_north[1], True), turn_row(down_w, of_south[0], True)]
        return [pre_grad[k] + inside[k] + beyond[k] + edges(rims, k) for k in range(2)]

    grad = spread_back(pre_grad, inside, up_w, down_w, sides_w)
    up_grad = (
        up + inner_row(up_w, tile_in[2, 0, 0]) + to_north + edges(swap_sides(turned_in[0, 0], turned_in[1, 0]), 1)
    )
    down_grad = (
        down + inner_row(down_w, tile_in[2, 1, 1]) + to_south + edges(swap_sides(turned_in[2, 0], turned_in[3, 0]), 0)
    )
    ends = ends_back((turned_in[0, 1], turned_in[1, 1]), (turned_in[2, 1], turned_in[3, 1]))
    sides_grad = sides + nearer + pltpu.roll(sides_w, 64, 1) - 4.0 * sides_w + own_turned + ends
    outer_cot = jnp.concatenate([up_grad, down_grad, unfold(sides_grad)], axis=1).astype(BF16)
    pre_grad, before = own_back(SUBSTEPS - 2, grad)
    back = network_back(outer_cot, outer_slope[...])[2]
    up_w = far_coef[0] * (up_grad + back[:, :X])
    down_w = far_coef[1] * (down_grad + back[:, X : 2 * X])
    sides_w = side_coef * (sides_grad + fold(back[:, 2 * X :]))
    grad = spread_back(pre_grad, inner([coef_ref[k] * pre_grad[k] for k in range(2)]), up_w, down_w, sides_w)

    def send_back(e, weighted):
        col_out[e] = turn_pack(pack(weighted), tables, True)
        for k in range(2):
            row_out[e, k] = turn_row(weighted[k], parts[k], True)
        return exchange(e, row_out.at[e, 0], row_out.at[e, 1])

    def come_back(e, pre_grad, inside):
        arrived(flights)
        sides = swap_sides(col_in[e, 0], col_in[e, 1])
        return [pre_grad[k] + inside[k] + row_in[e, k] + edges(sides, k) for k in range(2)]

    pre_grad, known = own_back(1, grad)
    weighted = [coef_ref[k] * pre_grad[k] for k in range(2)]
    flights = send_back(1, weighted)
    gather(before)
    gather(known)
    inside = inner(weighted)
    grad = come_back(1, pre_grad, inside)
    pre_grad, known = own_back(0, grad)
    folded, dw_in, dw_out = gather(known)

    dbias = lax.dot_general(
        jnp.ones((8, X), F32), folded, (((1,), (1,)), ((), ())),
        preferred_element_type=F32, precision=lax.Precision.HIGHEST,
    )
    blank = jnp.zeros((8, X), F32)
    for i in range(4):
        cut = slice(X * i, X * i + X)
        mine[0, i] = jnp.concatenate([dw_in[:, cut], blank, blank], axis=0)
        mine[1, i] = jnp.concatenate([dw_out[:, cut], dbias[:, cut], blank], axis=0)
    core_flights = []
    for n, j in enumerate((2, 1, 3, 0)):
        tile = (x + j) % 4
        core_flights.append(
            start(remote(mine.at[1 - core, tile], half_in.at[j], core_send.at[n], core_recv.at[n], at_core()))
        )

    weighted = [coef_ref[k] * pre_grad[k] for k in range(2)]
    flights = send_back(0, weighted)
    inside = inner(weighted)

    x_flights = []
    for n, j in enumerate((2, 1, 3, 0)):
        tile = (x + j) % 4
        core_flights[n].wait_recv()
        if j:
            half_in[j] = half_in[j] + mine[core, tile]
            x_flights.append(start(remote(half_in.at[j], x_in.at[j - 1], xs_send.at[j - 1], xs_recv.at[j - 1], at_x(j))))
        else:
            total = half_in[0] + mine[core, tile]
    for flight in x_flights:
        flight.wait_recv()
    tile_ref[...] = (total + x_in[0] + x_in[1] + x_in[2]).reshape(OWNERS, PIECE, X)

    def y_copy(j):
        return remote(tile_ref.at[(y + j) % 8], y_in.at[j - 1], ys_send.at[j - 1], ys_recv.at[j - 1], at_y(j))

    def z_copy(j):
        return remote(piece_ref, z_in.at[z], zs_send.at[j - 1], zs_recv.at[j - 1], at_z(j))

    order = (4, 3, 5, 2, 6, 1, 7)
    for j in order:
        @pl.when((y + j) % 8 < OWNERS)
        def _():
            y_copy(j).start()

    grad = come_back(0, pre_grad, inside)
    for k in range(2):
        grad_vmem[k] = grad[k]
    results[1].start()
    for copy in copies:
        copy.wait_send()
    copies.clear()

    @pl.when(y < OWNERS)
    def _():
        part = tile_ref[y]
        for j in range(1, 8):
            came = y_in.at[j - 1]
            remote(came, came, ys_send.at[j - 1], ys_recv.at[j - 1], at_y(j)).wait_recv()
            part = part + y_in[j - 1]
        piece_ref[...] = part
        z_in[z] = part
        for j in order:
            z_copy(j).start()
        for j in order:
            z_copy(j).wait_recv()
        whole = z_in[0]
        for i in range(1, 8):
            whole = whole + z_in[i]
        all_ref[x, y] = whole * factor

    def yg_copy(j):
        return remote(all_ref.at[x, y], all_ref.at[x, y], yg_send.at[j - 1], yg_recv.at[j - 1], at_y(j))

    def xg_copy(j, owner):
        piece = all_ref.at[x, owner]
        return remote(piece, piece, xg_send.at[j - 1, owner], xg_recv.at[j - 1, owner], at_x(j))

    @pl.when(y < OWNERS)
    def _():
        for j in order:
            yg_copy(j).start()

    for j in (0, 1, 7, 2, 6, 3, 5, 4):
        owner = (y - j + 8) % 8

        @pl.when(owner < OWNERS)
        def _():
            if j:
                came = all_ref.at[x, owner]
                remote(came, came, yg_send.at[j - 1], yg_recv.at[j - 1], at_y(j)).wait_recv()
            for i in (2, 1, 3):
                xg_copy(i, owner).start()

        if j == 0:
            for i in order:
                @pl.when((y + i) % 8 < OWNERS)
                def _():
                    y_copy(i).wait_send()

            @pl.when(y < OWNERS)
            def _():
                for i in order:
                    z_copy(i).wait_send()

    def hand_over(n, tile):
        pltpu.make_async_copy(all_ref.at[tile], sums_ref.at[core, tile], keep_sem.at[n]).start()
        return start(remote(all_ref.at[tile], sums_ref.at[core, tile], cg_send.at[n], cg_recv.at[n], at_core()))

    cg_flights = [hand_over(0, x)]
    for j in (1, 3, 2):
        for owner in range(OWNERS):
            xg_copy(j, owner).wait_recv()
        cg_flights.append(hand_over(j, (x - j + 4) % 4))
    for j in range(1, 4):
        for owner in range(OWNERS):
            xg_copy(j, owner).wait_send()

    @pl.when(y < OWNERS)
    def _():
        for j in order:
            yg_copy(j).wait_send()

    for result in results:
        result.wait()
    for flight in cg_flights:
        flight.wait_recv()
    for j in range(4):
        tile = (x - j + 4) % 4
        pltpu.make_async_copy(all_ref.at[tile], sums_ref.at[core, tile], keep_sem.at[j]).wait()
    for copy in copies:
        copy.wait_send()


def place_kernel(final_ref, grad_ref, sums_ref, *outs):
    outs[0][...] = final_ref[...]
    outs[1][...] = grad_ref[...]
    for i in range(4):
        cut = slice(X * i, X * i + X)
        outs[2][:, cut] = sums_ref[0, i, :C]
        outs[3][:, cut] = sums_ref[1, i, :C]
        outs[4][:, cut] = sums_ref[1, i, C : C + 1]


def shards(state, kappa, tile_face, seam_turn, face_rate, w_in, bias_in, w_out, cotangent):
    vmem = pl.BlockSpec(memory_space=pltpu.VMEM)
    hbm = pl.BlockSpec(memory_space=pltpu.HBM)
    operands = (tile_face, seam_turn, state, cotangent, kappa, face_rate, w_in, bias_in[None], w_out.T)
    steps = 2
    dma = lambda *shape: pltpu.SemaphoreType.DMA(shape)
    all_columns = lax.axis_size("rep") * lax.axis_size("ty") * lax.axis_size("tx") * 2 * X
    final, grad, sums = pl.pallas_call(
        functools.partial(step_kernel, 1.0 / math.sqrt(all_columns)),
        out_shape=(
            jax.ShapeDtypeStruct(state.shape, F32),
            jax.ShapeDtypeStruct(state.shape, F32),
            jax.ShapeDtypeStruct((2, 4, OWNERS, PIECE, X), F32),
        ),
        in_specs=[hbm] * 9,
        out_specs=(hbm, hbm, hbm),
        scratch_shapes=[
            *[pltpu.VMEM(operand.shape, operand.dtype) for operand in operands],
            dma(9),
            pltpu.VMEM((HID, KA), BF16),
            pltpu.VMEM((HID, C), BF16),
            pltpu.VMEM((2, C, X), F32),
            pltpu.VMEM((SUBSTEPS, C, 2 * X), BF16),
            pltpu.VMEM((SUBSTEPS, HID, 2 * X), BF16),
            pltpu.VMEM((SUBSTEPS, HID, 2 * X), F32),
            pltpu.VMEM((HID, X), F32),
            pltpu.VMEM((C, HID), F32),
            pltpu.VMEM((C, HID), F32),
            pltpu.VMEM((steps, 2, C, X), F32),
            pltpu.VMEM((steps, 8, X), F32),
            pltpu.VMEM((steps, 2, C, X), F32),
            pltpu.VMEM((steps, 2, 8, X), F32),
            pltpu.VMEM((2, C, X), F32),
            pltpu.VMEM((3, 2, 8, X), F32),
            pltpu.VMEM((3, 2, 2, C, X), F32),
            pltpu.VMEM((3, 2, 2, 8, X), F32),
            pltpu.VMEM((2, 4, 8, X), F32),
            pltpu.VMEM((2, 8, X), F32),
            pltpu.VMEM((4, 2, 8, X), F32),
            pltpu.VMEM((2, 2, C, X), F32),
            pltpu.VMEM((2, 8, X), F32),
            pltpu.VMEM((4, 2, 8, X), F32),
            pltpu.VMEM((HID, 3 * X), F32),
            pltpu.VMEM((2, 4, RED, X), F32),
            pltpu.VMEM((4, RED, X), F32),
            pltpu.VMEM((3, RED, X), F32),
            pltpu.VMEM((OWNERS, PIECE, X), F32),
            pltpu.VMEM((7, PIECE, X), F32),
            pltpu.VMEM((PIECE, X), F32),
            pltpu.VMEM((8, PIECE, X), F32),
            pltpu.VMEM((4, OWNERS, PIECE, X), F32),
            pltpu.VMEM((2, C, X), F32),
            pltpu.VMEM((2, C, X), F32),
            dma(steps, 2), dma(steps, 2), dma(steps, 2), dma(steps, 2), dma(3, 8), dma(3, 8), dma(4), dma(4),
            dma(4), dma(4), dma(3), dma(3), dma(7), dma(7), dma(7), dma(7),
            dma(7), dma(7), dma(3, OWNERS), dma(3, OWNERS), dma(4), dma(4), dma(4), dma(2),
        ],
        compiler_params=pltpu.CompilerParams(
            collective_id=0, has_side_effects=True, vmem_limit_bytes=62 << 20
        ),
        name="training_step",
    )(*operands)
    final, grad, total_in, total_out, total_bias = pl.pallas_call(
        place_kernel,
        out_shape=(
            jax.ShapeDtypeStruct(state.shape, F32),
            jax.ShapeDtypeStruct(state.shape, F32),
            jax.ShapeDtypeStruct((C, HID), F32),
            jax.ShapeDtypeStruct((C, HID), F32),
            jax.ShapeDtypeStruct((1, HID), F32),
        ),
        name="place_results",
    )(final, grad, sums.reshape(2, 4, RED, X))
    return final, grad, total_in, total_out.T, total_bias.reshape(HID)


def solution(mesh):
    placed = (
        P("rep", "ty", None, "tx"),
        P("ty", "tx"),
        P("ty", "tx"),
        P("ty", "tx", None),
        P(),
        P(),
        P(),
        P(),
        P("rep", "ty", None, "tx"),
    )
    return jax.shard_map(
        shards,
        mesh=mesh,
        in_specs=placed,
        out_specs=(P("rep", "ty", None, "tx"), P("rep", "ty", None, "tx"), P(), P(), P()),
        check_vma=False,
    )
```

time: 540 us -> 66 us (0.12)
  waiting for transfers between devices: 294 us -> 0 us
  blocking collectives: 97.9 us -> 0 us
  starting transfers between devices: 83.8 us -> 0 us
  Pallas kernels: 0 us -> 64.5 us
  between operations: 26.8 us -> 1.29 us
  local copies, waits for them, and re-layouts: 14.1 us -> 0 us
  matrix products: 11.4 us -> 0 us
  other arithmetic: 9.5 us -> 0 us
    psum x1 -> x0, waiting for transfers between devices: 259 us -> none  [shards(): lax.psum((total_in, total_out, total_bias), ('rep', 'ty', 'tx'))]
    psum x1 -> x0, blocking collectives: 97.9 us -> none  [shards(): lax.psum((total_in, total_out, total_bias), ('rep', 'ty', 'tx'))]
    ppermute x32 -> x0, starting transfers between devices: 83.7 us -> none  [the longest x16 49.4 us: extended(): after = lax.ppermute(first, axis, down)]
    pallas_call x0 -> x2, Pallas kernels: none -> 64.5 us  [the longest x1 62.6 us: shards(): pl.pallas_call(functools.partial(step_kernel, 1.0 / math.sqrt(all_columns...]
    ppermute x32 -> x0, waiting for transfers between devices: 34.6 us -> none  [the longest x16 29.3 us: extended(): before = lax.ppermute(last, axis, up)]
    dot_general x25 -> x0, matrix products: 11.4 us -> none  [the longest x4 3.46 us: column_backward(): jnp.einsum('hc,ycx->yhx', w_out, cot_b, preferred_element_type=jnp.float32)]
    slice x68 -> x0, local copies, waits for them, and re-layouts: 5.77 us -> none  [the longest x5 1.46 us: laplace(): eastern = turn_strip(padded[1:-1, :, -1].T, turns[3], False)]
  transfers between devices with their start and end apart: 33 -> 0, of which waited for: 18 -> 0; matrix products, arithmetic and copies ran while one was open for 1% -> 0% of each run, Pallas kernels for 0% -> 0%
where the time goes in v1:
time: 66 us; the launch traced here: 65.8 us
  Pallas kernels  64.5 us (98%)
  between operations  1.29 us (2%)
    pallas_call x1, Pallas kernels, shards(): pl.pallas_call(functools.partial(step_kernel, 1.0 / math.sqrt(all_columns...  62.6 us
    pallas_call x1, Pallas kernels, shards(): pl.pallas_call(place_kernel, out_shape=(jax.ShapeDtypeStruct(state.shape,...  1.87 us

profile of v1, /device:TPU:1, one launch (start us, length us, event | category | flops | bytes accessed | tf_op | source)
XLA Modules:
  0.0 65.8 jit_solution(2582502319621881515)
XLA Ops:
  1.3 62.6 %training_step.1 = (f32[1,2,80,128]{3,2,1,0:T(8,128)}, f32[1,2,80,128]{3,2,1,0:T(8,128)}, f32[2,4,6,16,128]{4,3,2,1,0:T(8,128)}) custom-call(s32[1,1]{1,0:T(1,128)S(6)} %copy.14.refs_0_, s32[1,1,4]{2,1,0:T(1,128)} %refs_1_.1, f32[1,2,80,128]{3,2,1,0:T(8,128)} %refs_2_.1, f32[1,2,80,128]{3,2,1,0:T(8,128)} %refs_3_.1, f32[2,128]{1,0:T(2,128)} %refs_4_.1, ...), custom_call_target="tpu_custom_call" | custom-call | tf_op jit(solution)/shard_map/training_step/pallas_call | solution.py:652
  63.9 1.9 %place_results.1 = (f32[1,2,80,128]{3,2,1,0:T(8,128)}, f32[1,2,80,128]{3,2,1,0:T(8,128)}, f32[80,512]{1,0:T(8,128)}, f32[80,512]{1,0:T(8,128)}, f32[1,512]{1,0:T(1,128)}) custom-call(f32[1,2,80,128]{3,2,1,0:T(8,128)} %get-tuple-element.13.final_ref, f32[1,2,80,128]{3,2,1,0:T(8,128)} %get-tuple-element.14.grad_ref, f32[2,4,96,128]{3,2,1,0:T(8,128)} %bitcast.5), custom_call_target="tpu_custom_call" | custom-call | tf_op jit(solution)/shard_map/place_results/pallas_call | solution.py:707
